TPU v7x, 32 devices: a whole 2x2x4 slice. The times are simulated.
32 devices in a mesh: ctx: 4 (over y, x), ch: 8 (over z, core).
Axes of the slice: x: 2, y: 2, z: 4, core: 2. Of those that a mesh axis runs over, the one named last changes fastest.
Arguments:
- streams_in: bfloat16 [3, 4096, 8192], P(None, 'ctx', 'ch'), may hold values from -6 to 6
- out_grad: bfloat16 [4096, 8192], P('ctx', 'ch'), may hold values from -6 to 6
- decay_rate: float32 [8192, 16], P('ch'), may hold values from 2.4414063e-05 to 0.03
- residue: float32 [8192, 16], P('ch'), may hold values from -1.5 to 1.5
- short_filter: float32 [3, 512, 3], replicated, may hold values from -2.5 to 2.5
Outputs:
- layer_out: bfloat16 [4096, 8192], P('ctx', 'ch')
- streams_grad: bfloat16 [3, 4096, 8192], P(None, ('ctx', 'ch'))
All inputs are finite; a program needn't handle non-finite values.
Results may differ from a plain program's by a relative error of at most 0.014.
Values may be sent and summed in bfloat16 or wider, within the bound.
A program may use at most 192 MiB of HBM per device.

v0:
```python
import jax
import jax.numpy as jnp
from jax import lax
from jax.sharding import PartitionSpec as P

GROUP_SIZE = 16
TAPS = 3
BLOCK = 128


highest = lax.Precision.HIGHEST


def shifted(block, axis, distance):
    devices = range(lax.axis_size(axis))
    route = [(i - distance, i) for i in devices if i - distance in devices]
    return lax.ppermute(block, axis, route)


def entering(array, axis, join, neutral, backward):
    count = lax.axis_size(axis)
    place = lax.axis_index(axis)
    ahead = count - 1 - place if backward else place
    gathered = jax.tree.map(
        lambda a, kind: lax.all_gather(a.astype(kind), axis), array, (jnp.bfloat16, jnp.bfloat16)
    )
    state = jax.tree.map(lambda a, e: jnp.zeros_like(a) + jnp.asarray(e, a.dtype), array, neutral)

    def one(hop, state):
        source = count - 1 - hop if backward else hop
        return join(
            state,
            jax.tree.map(
                lambda a, own: lax.dynamic_index_in_dim(a, source, 0, False).astype(own.dtype),
                gathered,
                array,
            ),
        )

    return lax.fori_loop(0, ahead, one, state)


def filter_tables(decay_rate, residue):
    weight_amp = residue * jnp.sqrt(2.0 * decay_rate)
    lag_index = jnp.arange(BLOCK).astype(decay_rate.dtype)
    powers = jnp.exp(-decay_rate[:, None, :] * lag_index[None, :, None])
    filter_lags = jnp.sum(weight_amp[:, None, :] * powers, axis=2)
    offsets = jnp.arange(BLOCK)[:, None] - jnp.arange(BLOCK)[None, :]
    toeplitz = jnp.where(offsets[None] >= 0, filter_lags[:, jnp.maximum(offsets, 0)], 0.0).astype(
        jnp.bfloat16
    )
    one_step = jnp.exp(-decay_rate)[:, None, :]
    emit_forward = powers[:, ::-1, :]
    inject_forward = weight_amp[:, None, :] * powers * one_step
    inject_backward = weight_amp[:, None, :] * powers[:, ::-1, :] * one_step
    return (toeplitz, emit_forward, powers, inject_forward, inject_backward)


def short_forward(padded, filters, length):
    summed = [
        filters[:, None, :, shift_index]
        * padded[:, TAPS - 1 - shift_index : TAPS - 1 - shift_index + length, :].astype(jnp.float32)
        for shift_index in range(TAPS)
    ]
    return sum(summed[1:], summed[0])


def short_backward(padded, filters, length):
    summed = [
        filters[:, None, :, shift_index]
        * padded[:, shift_index : shift_index + length, :].astype(jnp.float32)
        for shift_index in range(TAPS)
    ]
    return sum(summed[1:], summed[0])


def combine_pair(earlier_part, later_part):
    return (earlier_part[0] * later_part[0], later_part[0] * earlier_part[1] + later_part[1])


def shards(streams_in, out_grad, decay_rate, residue, short_filter):
    length = streams_in.shape[1]
    chan_count = streams_in.shape[2]
    block_count = length // BLOCK
    toeplitz, emit_forward, emit_backward, inject_forward, inject_backward = filter_tables(
        decay_rate, residue
    )
    groups_here = chan_count // GROUP_SIZE
    local_filter = lax.dynamic_slice_in_dim(
        short_filter, lax.axis_index("ch") * groups_here, groups_here, 1
    )
    filters = jnp.repeat(local_filter, GROUP_SIZE, axis=1)
    prior_rows = shifted(streams_in[:, length - (TAPS - 1) :, :], "ctx", 1)
    features = short_forward(
        jnp.concatenate([prior_rows, streams_in], axis=1), filters, length
    ).astype(jnp.bfloat16)
    query_part = features[0].astype(jnp.float32)
    key_part = features[1].astype(jnp.float32)
    value_part = features[2].astype(jnp.float32)
    product = (key_part * value_part).astype(jnp.bfloat16)
    out_wide = out_grad.astype(jnp.float32)
    adjoint = (out_wide * query_part).astype(jnp.bfloat16)
    blocks = product.reshape(block_count, BLOCK, chan_count)
    adj_blocks = adjoint.reshape(block_count, BLOCK, chan_count)
    inside = jnp.einsum("cij,kjc->kic", toeplitz, blocks, preferred_element_type=jnp.float32)
    inside_back = jnp.einsum(
        "cij,kic->kjc", toeplitz, adj_blocks, preferred_element_type=jnp.float32
    )
    emitted = jnp.einsum(
        "kjc,cjn->kcn", blocks.astype(jnp.float32), emit_forward, precision=highest
    )
    emitted_back = jnp.einsum(
        "kic,cin->kcn", adj_blocks.astype(jnp.float32), emit_backward, precision=highest
    )
    block_pos = jnp.arange(block_count)
    gap_blocks = (block_pos[:, None] - 1 - block_pos[None, :]).astype(jnp.float32)
    earlier_mask = block_pos[None, :] < block_pos[:, None]
    prefix_weight = jnp.where(
        earlier_mask[None, None],
        jnp.exp(-decay_rate[:, :, None, None] * BLOCK * jnp.maximum(gap_blocks, 0.0)[None, None]),
        0.0,
    )
    local_before = jnp.einsum("cnkl,lcn->kcn", prefix_weight, emitted, precision=highest)
    local_after = jnp.einsum("cnlk,lcn->kcn", prefix_weight, emitted_back, precision=highest)
    lead_decay = jnp.exp(-decay_rate[None] * BLOCK * block_pos.astype(jnp.float32)[:, None, None])
    span_emit = jnp.sum(lead_decay[::-1] * emitted, axis=0)
    span_back = jnp.sum(lead_decay * emitted_back, axis=0)
    span_decay = jnp.exp(-decay_rate * length)
    identity = (jnp.ones_like(span_decay), jnp.zeros_like(span_emit))
    _, incoming = entering((span_decay, span_emit), "ctx", combine_pair, identity, False)
    _, outgoing = entering((span_decay, span_back), "ctx", combine_pair, identity, True)
    state_before = local_before + lead_decay * incoming[None]
    state_after = local_after + lead_decay[::-1] * outgoing[None]
    long_out = (
        inside + jnp.einsum("cin,kcn->kic", inject_forward, state_before, precision=highest)
    ).reshape(length, chan_count)
    long_grad = (
        inside_back + jnp.einsum("cjn,kcn->kjc", inject_backward, state_after, precision=highest)
    ).reshape(length, chan_count)
    layer_out = (query_part * long_out).astype(jnp.bfloat16)
    stream_grads = jnp.stack(
        [out_wide * long_out, long_grad * value_part, long_grad * key_part]
    ).astype(jnp.bfloat16)
    token_grads = lax.all_to_all(stream_grads, "ch", split_axis=1, concat_axis=2, tiled=True)
    token_rows = token_grads.shape[1]
    all_filters = jnp.repeat(short_filter, GROUP_SIZE, axis=1)
    following = shifted(token_grads[:, : TAPS - 1, :], ("ctx", "ch"), -1)
    streams_grad = short_backward(
        jnp.concatenate([token_grads, following], axis=1), all_filters, token_rows
    ).astype(jnp.bfloat16)
    return (layer_out, streams_grad)


def solution(mesh):
    return jax.shard_map(
        shards,
        mesh=mesh,
        in_specs=(P(None, "ctx", "ch"), P("ctx", "ch"), P("ch", None), P("ch", None), P()),
        out_specs=(P("ctx", "ch"), P(None, ("ctx", "ch"), None)),
        check_vma=False,
    )
```

profile of v0, /device:TPU:27, one launch (start us, length us, event | category | flops | bytes accessed | tf_op | source)
XLA Modules:
  0.0 590.2 jit_solution(4454442164257327484)
XLA Ops:
  0.6 0.8 slice.47
  1.4 3.1 collective-permute-start
  4.7 0.8 constant_dynamic-slice_fusion
  5.5 0.1 broadcast_in_dim.26
  5.6 0.2 reshape.151
  5.8 0.9 exponential_convert_fusion
  6.7 0.2 copy.101
  6.9 0.2 copy.100
  7.2 0.1 convert_maximum_fusion
  7.2 13.2 %multiply_exponential_fusion = (f32[1024,128,16]{1,2,0:T(8,128)}, bf16[1024,128]{1,0:T(8,128)(2,1)S(1)}) fusion(f32[128]{0:T(128)S(1)} %iota_convert_fusion.1, f32[1024,16]{1,0:T(8,128)S(1)} %copy.101, f32[1024,16]{1,0:T(8,128)S(1)} %copy.100), kind=kLoop, calls=%fused_computation.16 | loop fusion | flops 6160384 | bytes 8782336 | tf_op jit(solution)/shard_map/exp | solution.py:46
  20.4 5.8 all-gather
  26.3 0.1 copy.102
  26.4 69.9 %gather_fusion = bf16[16384,1024]{1,0:T(8,128)(2,1)} fusion(bf16[1024,128]{0,1:T(8,128)(2,1)S(1)} %copy.102, s32[16384]{0:T(1024)S(1)} %bitcast_clamp_fusion), kind=kCustom, calls=%fused_computation | custom fusion | bytes 67174400 | tf_op jit(solution)/shard_map/gather | solution.py:49
  96.3 46.0 %copy.103 = bf16[128,128,1024]{1,0,2:T(8,128)(2,1)} copy(bf16[128,128,1024]{2,1,0:T(8,128)(2,1)} %bitcast.110) | data formatting | bytes 67108864 | tf_op jit(solution)/shard_map/gather | solution.py:49
  142.3 13.1 %rev.8 = f32[1024,128,16]{1,2,0:T(8,128)} reverse(f32[1024,128,16]{1,2,0:T(8,128)} %get-tuple-element.199), dimensions={1} | reverse | bytes 16777216 | tf_op jit(solution)/shard_map/rev | solution.py:53
  155.4 1.0 copy.111
  156.5 1.0 copy.106
  157.5 10.9 %add_convert_fusion.1 = bf16[3,1024,1024]{2,1,0:T(8,128)(2,1)S(1)} fusion(bf16[3,1024,1024]{2,1,0:T(8,128)(2,1)} %param.9, bf16[3,2,1024]{2,1,0:T(2,128)(2,1)S(1)} %collective-permute-done, f32[3,1024]{1,0:T(4,128)S(1)} %get-tuple-element.215, f32[3,1024]{1,0:T(4,128)S(1)} %get-tuple-element.216, f32[3,1024]{1,0:T(4,128)S(1)} %bitcast.122), kind=kLoop, calls=%fused_computation.10 | loop fusion | flops 47185920 | bytes 12632064 | tf_op jit(solution)/shard_map/convert_element_type | solution.py:96
  168.4 2.7 copy-done.1
  171.1 1.0 fusion.18
  172.1 2.9 copy.114
  175.0 15.0 %fusion.19 = (bf16[1024,16]{1,0:T(8,128)(2,1)S(1)}, f32[8,1024,16]{2,0,1:T(8,128)}, f32[1024,16,8]{1,2,0:T(8,128)}) fusion(f32[8]{0:T(128)S(1)} %iota_convert_fusion, f32[1024,16]{1,0:T(8,128)} %copy.106, bf16[8,128,1024]{1,0,2:T(8,128)(2,1)} %copy.114, f32[128]{0:T(128)S(1)} %iota_convert_fusion.1, f32[1024,16]{1,0:T(8,128)S(1)} %copy.101), kind=kOutput, calls=%fused_computation.39 | convolution fusion | flops 203800576 | bytes 3310112 | tf_op jit(solution)/shard_map/kic,cin->kcn/dot_general | solution.py:112
  189.9 3.0 copy.152
  192.9 0.9 multiply_reduce_fusion.1
  193.8 2.7 copy.138
  196.6 6.6 %rev.9 = f32[8,1024,16]{2,0,1:T(8,128)} reverse(f32[8,1024,16]{2,0,1:T(8,128)} %get-tuple-element.198), dimensions={0} | reverse | bytes 1048576 | tf_op jit(solution)/shard_map/rev | solution.py:126
  203.2 11.0 %all-gather.2 = bf16[4096,16]{1,0:T(8,128)(2,1)S(1)} all-gather(bf16[1024,16]{1,0:T(8,128)(2,1)S(1)} %get-tuple-element.197), channel_id=4, replica_groups=mesh['ctx'=4,'ch'=8] {'ctx'}, dimensions={0}, use_global_device_ids=true | all-gather | bytes 163840 | tf_op jit(solution)/shard_map/all_gather | solution.py:25
  214.2 0.3 copy.118
  214.5 0.6 while.27
  215.1 0.2 copy.119
  215.3 17.1 %fusion.1 = f32[1024,8,128]{2,1,0:T(8,128)} fusion(bf16[8,128,1024]{1,0,2:T(8,128)(2,1)} %copy.114, bf16[128,128,1024]{1,0,2:T(8,128)(2,1)} %copy.103, pred[128,128]{1,0:T(8,128)(4,1)S(1)} %subtract_compare_fusion), kind=kOutput, calls=%fused_computation.7 | convolution fusion | flops 285212672 | bytes 39862272 | tf_op jit(solution)/shard_map/cij,kic->kjc/dot_general | solution.py:106
  232.4 14.3 %add_bitcast_fusion = f32[8,128,1024]{1,0,2:T(8,128)} fusion(f32[1024,8,128]{2,1,0:T(8,128)} %fusion.1, f32[1024,128,16]{1,2,0:T(8,128)} %rev.8, f32[1024,16]{1,0:T(8,128)S(1)} %copy-done.10, f32[1024,16]{1,0:T(8,128)S(1)} %copy.100, f32[1024,16,8]{1,2,0:T(8,128)} %copy.138, f32[8,1024,16]{2,0,1:T(8,128)} %rev.9, f32[1024,16]{1,0:T(8,128)S(1)} %copy.119), kind=kOutput, calls=%fused_computation.45 | convolution fusion | flops 206831616 | bytes 18022400 | tf_op jit(solution)/shard_map/cjn,kcn->kjc/dot_general | solution.py:138
  246.7 5.4 copy.144
  252.1 7.9 %fusion.15 = (bf16[1,1024,1024]{2,1,0:T(8,128)(2,1)}, bf16[1,1024,1024]{2,1,0:T(8,128)(2,1)}, bf16[1,1024,1024]{2,1,0:T(8,128)(2,1)}) fusion(bf16[3,1024,1024]{2,1,0:T(8,128)(2,1)} %copy-done.1, f32[1,1024,1024]{2,1,0:T(8,128)} %bitcast.113), kind=kLoop, calls=%fused_computation.33 | loop fusion | flops 8388608 | bytes 14680064 | tf_op jit(solution)/shard_map/convert.6
  260.0 3.4 copy.104
  263.4 22.3 %fusion.3 = f32[1024,8,128]{2,1,0:T(8,128)} fusion(bf16[8,128,1024]{1,0,2:T(8,128)(2,1)S(1)} %copy.104, bf16[128,128,1024]{1,0,2:T(8,128)(2,1)} %copy.103, pred[128,128]{1,0:T(8,128)(4,1)S(1)} %subtract_compare_fusion), kind=kOutput, calls=%fused_computation.8 | convolution fusion | flops 285212672 | bytes 39862272 | tf_op jit(solution)/shard_map/cij,kjc->kic/dot_general | solution.py:105
  285.6 12.4 %fusion.20 = (bf16[1024,16]{1,0:T(8,128)(2,1)S(1)}, f32[1024,16,8]{1,2,0:T(8,128)}) fusion(f32[8,1024,16]{2,0,1:T(8,128)S(1)} %copy-done, f32[1024,128,16]{1,2,0:T(8,128)} %rev.8, bf16[8,128,1024]{1,0,2:T(8,128)(2,1)S(1)} %copy.104), kind=kOutput, calls=%fused_computation.42 | convolution fusion | flops 201572352 | bytes 11567104 | tf_op jit(solution)/shard_map/kjc,cjn->kcn/dot_general | solution.py:109
  298.1 3.0 copy.151
  301.1 1.8 multiply_reduce_fusion.2
  302.9 2.7 copy.131
  305.6 10.2 %all-gather.1 = bf16[4096,16]{1,0:T(8,128)(2,1)S(1)} all-gather(bf16[1024,16]{1,0:T(8,128)(2,1)S(1)} %get-tuple-element.213), channel_id=3, replica_groups=mesh['ctx'=4,'ch'=8] {'ctx'}, dimensions={0}, use_global_device_ids=true | all-gather | bytes 163840 | tf_op jit(solution)/shard_map/all_gather | solution.py:25
  315.8 0.3 copy.109
  316.1 0.1 while.26
  316.2 0.2 copy.110
  316.4 16.0 %add_bitcast_fusion.1 = f32[8,128,1024]{1,0,2:T(8,128)} fusion(f32[1024,8,128]{2,1,0:T(8,128)} %fusion.3, f32[1024,16]{1,0:T(8,128)S(1)} %copy-done.11, f32[128]{0:T(128)S(1)} %iota_convert_fusion.1, f32[1024,16]{1,0:T(8,128)S(1)} %copy-done.9, f32[1024,16]{1,0:T(8,128)S(1)} %copy-done.7, f32[1024,16,8]{1,2,0:T(8,128)} %copy.131, ...), kind=kOutput, calls=%fused_computation.47 | convolution fusion | flops 209059840 | bytes 9241120 | tf_op jit(solution)/shard_map/cin,kcn->kic/dot_general | solution.py:135
  332.4 5.6 copy.143
  338.0 5.7 fusion.16
  343.7 3.1 pad_maximum_fusion.1
  346.8 11.4 %copy.122 = bf16[3,1024,1024]{2,0,1:T(4,128)(2,1)} copy(bf16[3,1024,1024]{2,1,0:T(8,128)(2,1)} %pad_maximum_fusion.1) | data formatting | bytes 12582912 | tf_op jit(solution)/shard_map/stack | solution.py:141
  358.2 12.1 %all-to-all-start = ((bf16[3,1024,1024]{2,0,1:T(4,128)(2,1)}), bf16[3,1024,1024]{2,0,1:T(4,128)(2,1)}, u32[]{:S(2)}, u32[]{:S(2)}) async-start(bf16[3,1024,1024]{2,0,1:T(4,128)(2,1)} %copy.122), calls=%async_computation | async-start | bytes 16777216 | tf_op jit(solution)/shard_map/all_to_all | solution.py:144
  370.3 0.7 broadcast_in_dim.36
  371.0 1.3 reshape.153
  372.3 0.2 fusion.41
  372.5 0.1 copy.164
  372.6 0.1 copy_bitcast_fusion.1
  372.8 178.8 %all-to-all-done = bf16[3,1024,1024]{2,0,1:T(4,128)(2,1)} async-done(((bf16[3,1024,1024]{2,0,1:T(4,128)(2,1)}), bf16[3,1024,1024]{2,0,1:T(4,128)(2,1)}, u32[]{:S(2)}, u32[]{:S(2)}) %all-to-all-start) | async-done | bytes 6291488 | tf_op jit(solution)/shard_map/all_to_all | solution.py:144
  551.6 10.7 %copy.123 = bf16[3,128,8,1024]{3,2,1,0:T(8,128)(2,1)} copy(bf16[3,128,8,1024]{3,0,1,2:T(4,128)(2,1)} %bitcast.26) | data formatting | bytes 12582912 | tf_op jit(solution)/shard_map/all_to_all | solution.py:144
  562.2 10.4 %all_to_all.16 = bf16[3,128,8192]{2,1,0:T(8,128)(2,1)} reshape(bf16[3,128,8,1024]{3,2,1,0:T(8,128)(2,1)} %copy.123) | data formatting | bytes 12582912 | tf_op jit(solution)/shard_map/all_to_all | solution.py:144
  572.7 1.2 slice.72
  573.9 2.5 collective-permute-start.1
  576.4 3.2 constant_dynamic-update-slice_fusion.1
  579.6 4.0 collective-permute-done.1
  583.6 0.1 constant_dynamic-update-slice_fusion
  583.7 6.1 %add_convert_fusion = bf16[3,128,8192]{2,1,0:T(8,128)(2,1)} fusion(bf16[3,128,8192]{2,1,0:T(8,128)(2,1)S(1)} %bitcast.112, bf16[3,130,8192]{2,1,0:T(8,128)(2,1)S(1)} %constant_dynamic-update-slice_fusion, f32[3,8192]{1,0:T(4,128)S(1)} %get-tuple-element.217, f32[3,8192]{1,0:T(4,128)S(1)} %get-tuple-element.218, f32[3,8192]{1,0:T(4,128)S(1)} %bitcast.120), kind=kLoop, calls=%fused_computation.9 | loop fusion | flops 28311552 | bytes 25460736 | tf_op jit(solution)/shard_map/convert_element_type | solution.py:150
  (50 shorter events, 0.3 us)
Async XLA Ops:
  1.4 156.0 %collective-permute-start = (bf16[3,2,1024]{2,1,0:T(2,128)(2,1)S(1)}, bf16[3,2,1024]{2,1,0:T(2,128)(2,1)S(1)}, u32[]{:S(2)}, u32[]{:S(2)}) collective-permute-start(bf16[3,2,1024]{2,1,0:T(2,128)(2,1)S(1)} %slice.47), channel_id=1, source_target_pairs={{0,8},{8,16},{16,24},{1,9},{9,17},{17,25},{2,10},{10,18},{18,26},{... | collective-permute-start | bytes 36872 | tf_op jit(solution)/shard_map/ppermute | solution.py:17
  6.7 186.2 %copy-start.12 = (f32[1024,16]{0,1:T(8,128)}, f32[1024,16]{0,1:T(8,128)S(1)}, u32[]{:S(2)}) copy-start(f32[1024,16]{0,1:T(8,128)S(1)} %get-tuple-element.205) | copy-start | bytes 196612
  6.9 168.1 %copy-start.8 = (f32[1024,16]{1,0:T(8,128)}, f32[1024,16]{1,0:T(8,128)S(1)}, u32[]{:S(2)}) copy-start(f32[1024,16]{1,0:T(8,128)S(1)} %copy.101) | copy-start | bytes 196612
  7.1 225.2 %copy-start.6 = (f32[1024,16]{1,0:T(8,128)}, f32[1024,16]{1,0:T(8,128)S(1)}, u32[]{:S(2)}) copy-start(f32[1024,16]{1,0:T(8,128)S(1)} %copy.100) | copy-start | bytes 196612
  157.5 13.6 %copy-start.2 = (bf16[1024,1024]{1,0:T(8,128)(2,1)S(1)}, bf16[1024,1024]{1,0:T(8,128)(2,1)}, u32[]{:S(2)}) copy-start(bf16[1024,1024]{1,0:T(8,128)(2,1)} %param.10) | copy-start | bytes 6291460
  168.4 2.7 copy-start.1
  215.3 17.1 %copy-start.10 = (f32[1024,16]{1,0:T(8,128)S(1)}, f32[1024,16]{1,0:T(8,128)}, u32[]{:S(2)}) copy-start(f32[1024,16]{1,0:T(8,128)} %copy.111) | copy-start | bytes 196612
  263.4 22.3 %copy-start = (f32[8,1024,16]{2,0,1:T(8,128)S(1)}, f32[8,1024,16]{2,0,1:T(8,128)}, u32[]{:S(2)}) copy-start(f32[8,1024,16]{2,0,1:T(8,128)} %rev.9) | copy-start | bytes 1572868
  298.1 3.0 copy-start.13
  302.9 13.5 %copy-start.7 = (f32[1024,16]{1,0:T(8,128)S(1)}, f32[1024,16]{1,0:T(8,128)}, u32[]{:S(2)}) copy-start(f32[1024,16]{1,0:T(8,128)} %copy-done.6) | copy-start | bytes 196612
  302.9 13.5 %copy-start.9 = (f32[1024,16]{1,0:T(8,128)S(1)}, f32[1024,16]{1,0:T(8,128)}, u32[]{:S(2)}) copy-start(f32[1024,16]{1,0:T(8,128)} %copy-done.8) | copy-start | bytes 196612
  302.9 13.5 %copy-start.11 = (f32[1024,16]{1,0:T(8,128)S(1)}, f32[1024,16]{1,0:T(8,128)}, u32[]{:S(2)}) copy-start(f32[1024,16]{1,0:T(8,128)} %copy.111) | copy-start | bytes 196612
  332.4 5.6 copy-start.3
  338.0 5.7 copy-start.4
  338.0 5.7 copy-start.5
  358.2 12.1 %copy-start.14 = (f32[3,512,3]{1,2,0:T(4,128)S(1)}, f32[3,512,3]{1,2,0:T(4,128)}, u32[]{:S(2)}) copy-start(f32[3,512,3]{1,2,0:T(4,128)} %param.13) | copy-start | bytes 55300
  358.2 193.4 %all-to-all-start = ((bf16[3,1024,1024]{2,0,1:T(4,128)(2,1)}), bf16[3,1024,1024]{2,0,1:T(4,128)(2,1)}, u32[]{:S(2)}, u32[]{:S(2)}) async-start(bf16[3,1024,1024]{2,0,1:T(4,128)(2,1)} %copy.122), calls=%async_computation | async-start | bytes 16777216 | tf_op jit(solution)/shard_map/all_to_all | solution.py:144
  572.7 11.0 %slice-start = ((s8[6291456]{0:T(1024)(128)(4,1)}), s8[4194304]{0:T(1024)(128)(4,1)S(1)}, s32[]{:S(2)}) async-start(s8[6291456]{0:T(1024)(128)(4,1)} %bitcast.111), calls=%async_computation.1 | async-start | bytes 8388608
  573.9 9.8 %slice-start.1 = ((s8[6291456]{0:T(1024)(128)(4,1)}), s8[2097152]{0:T(1024)(128)(4,1)S(1)}, s32[]{:S(2)}) async-start(s8[6291456]{0:T(1024)(128)(4,1)} %bitcast.111), calls=%async_computation.2 | async-start | bytes 4194304
  573.9 9.7 %collective-permute-start.1 = (bf16[3,2,8192]{2,1,0:T(2,128)(2,1)S(1)}, bf16[3,2,8192]{2,1,0:T(2,128)(2,1)S(1)}, u32[]{:S(2)}, u32[]{:S(2)}) collective-permute-start(bf16[3,2,8192]{2,1,0:T(2,128)(2,1)S(1)} %slice.72), channel_id=1, source_target_pairs={{1,0},{2,1},{3,2},{4,3},{5,4},{6,5},{7,6},{8,7},{9,8},{10,9},{11,1... | collective-permute-start | bytes 294920 | tf_op jit(solution)/shard_map/ppermute | solution.py:17
where the time goes:
time: 602 us; the launch traced here: 590 us
  local copies, waits for them, and re-layouts  212 us (35%)
  waiting for transfers between devices  183 us (30%)
  matrix products  97 us (16%)
  other arithmetic  51.6 us (9%)
  blocking collectives  27 us (4%)
  starting transfers between devices  17.7 us (3%)
    all_to_all x1, waiting for transfers between devices, shards(): lax.all_to_all(stream_grads, 'ch', split_axis=1, concat_axis=2, tiled=True)  179 us
    gather x2, local copies, waits for them, and re-layouts, filter_tables(): filter_lags[:, jnp.maximum(offsets, 0)]  116 us
    all_gather x3, blocking collectives, entering(): lax.all_gather(a.astype(kind), axis)  27 us
    dot_general x1, matrix products, shards(): jnp.einsum('cij,kjc->kic', toeplitz, blocks, preferred_element_type=jnp.f...  22.3 us
    all_to_all x2, local copies, waits for them, and re-layouts, shards(): lax.all_to_all(stream_grads, 'ch', split_axis=1, concat_axis=2, tiled=True)  21.1 us
    dot_general x1, matrix products, shards(): jnp.einsum('cij,kic->kjc', toeplitz, adj_blocks, preferred_element_type=j...  17.1 us
    dot_general x1, matrix products, shards(): jnp.einsum('cin,kcn->kic', inject_forward, state_before, precision=highest)  16 us
    dot_general x1, matrix products, shards(): jnp.einsum('kic,cin->kcn', adj_blocks.astype(jnp.float32), emit_backward,...  15 us
  transfers between devices with their start and end apart: 3, of which 2 were waited for; matrix products, arithmetic and copies ran while one was open for 26% of the time, Pallas kernels for 0%

commit v1 on v0

v1 whole, which is shorter than its diff:
```python
import functools

import jax
import jax.numpy as jnp
from jax import lax
from jax.experimental import pallas as pl
from jax.experimental.pallas import tpu as pltpu
from jax.sharding import PartitionSpec as P

GROUP_SIZE = 16
TAPS = 3
BLOCK = 128
LANES = 128
ROWS = 8
ORDER = 16
STRIDE = 136
UNROLL = 4
MESH = pl.DeviceIdType.MESH
f32 = jnp.float32
bf16 = jnp.bfloat16


def spread(rows):
    return jnp.broadcast_to(rows[:, None, :], (rows.shape[0], ROWS, LANES))


def steps(body, carry, backward=False, count=BLOCK):
    def some(j, carry):
        for u in range(UNROLL):
            i = j * UNROLL + u
            carry = body(count - 1 - i if backward else i, carry)
        return carry

    return lax.fori_loop(0, count // UNROLL, some, carry)


def kernel(
    nctx, nch, groups,
    x_hbm, og_hbm, rate_ref, res_ref, filt_ref,
    lay_hbm, sgrad_hbm,
    xin, ogin, halo, xf, ogf, qt, kt, vt, ot, pt, at, ef, eb,
    st_send, st_recv, sg, nat, bsend, brecv, send, lay,
    in_sem, halo_send, halo_recv, st_ssem, st_rsem, b_ssem, b_rsem,
    out_ssem, out_rsem, own_sem, lay_sem,
):
    span = x_hbm.shape[1]
    chans = x_hbm.shape[2]
    token_rows = span // nch
    c = lax.axis_index("ctx")
    h = lax.axis_index("ch")

    def lanes(g):
        return pl.ds(pl.multiple_of(g * LANES, LANES), LANES)

    def x_copy(g):
        return pltpu.make_async_copy(x_hbm.at[:, :, lanes(g)], xin.at[g], in_sem.at[0, g])

    def og_copy(g):
        return pltpu.make_async_copy(og_hbm.at[:, lanes(g)], ogin.at[g], in_sem.at[1, g])

    def load(g, _):
        x_copy(g).start()
        og_copy(g).start()
        return 0

    lax.fori_loop(0, groups, load, 0)

    barrier = pltpu.get_barrier_semaphore()

    def greet_ch(k, _):
        pl.semaphore_signal(barrier, inc=1, device_id={"ch": lax.rem(h + k, nch)}, device_id_type=MESH)
        return 0

    def greet_ctx(k, _):
        pl.semaphore_signal(barrier, inc=1, device_id={"ctx": lax.rem(c + k, nctx)}, device_id_type=MESH)
        return 0

    lax.fori_loop(1, nctx, greet_ctx, 0)
    lax.fori_loop(1, nch, greet_ch, 0)
    pl.semaphore_wait(barrier, nch + nctx - 2)

    def halo_copy(g, target):
        return pltpu.make_async_remote_copy(
            src_ref=x_hbm.at[:, pl.ds(span - 16, 16), lanes(g)],
            dst_ref=halo.at[g],
            send_sem=halo_send.at[g],
            recv_sem=halo_recv.at[g],
            device_id={"ctx": target},
            device_id_type=MESH,
        )

    @pl.when(c < nctx - 1)
    def _():
        def go(g, _):
            halo_copy(g, c + 1).start()
            return 0

        lax.fori_loop(0, groups, go, 0)

    def state_copy(g, way, peer, slot):
        return pltpu.make_async_remote_copy(
            src_ref=st_send.at[g, way],
            dst_ref=st_recv.at[g, slot],
            send_sem=st_ssem.at[g, peer],
            recv_sem=st_rsem.at[g, slot],
            device_id={"ctx": peer},
            device_id_type=MESH,
        )

    def edge_copy(g, target):
        return pltpu.make_async_remote_copy(
            src_ref=bsend.at[g],
            dst_ref=brecv.at[g],
            send_sem=b_ssem.at[g],
            recv_sem=b_rsem.at[g],
            device_id={"ctx": target},
            device_id_type=MESH,
        )

    def out_copy(g, peer, source):
        first = pl.multiple_of(source * chans + g * LANES, LANES)
        return pltpu.make_async_remote_copy(
            src_ref=send.at[g, :, pl.ds(pl.multiple_of(peer * token_rows, token_rows), token_rows), :],
            dst_ref=sgrad_hbm.at[:, :, pl.ds(first, LANES)],
            send_sem=out_ssem.at[g, peer],
            recv_sem=out_rsem.at[g, source],
            device_id={"ch": peer},
            device_id_type=MESH,
        )

    def own_copy(g):
        first = pl.multiple_of(h * chans + g * LANES, LANES)
        return pltpu.make_async_copy(
            send.at[g, :, pl.ds(pl.multiple_of(h * token_rows, token_rows), token_rows), :],
            sgrad_hbm.at[:, :, pl.ds(first, LANES)],
            own_sem.at[g],
        )

    def lay_copy(g):
        return pltpu.make_async_copy(lay.at[g], lay_hbm.at[:, lanes(g)], lay_sem.at[g])

    sublane = lax.broadcasted_iota(jnp.int32, (ORDER, ROWS, LANES), 1)
    sublane_f = sublane.astype(f32)

    def tap(g, s, p):
        return jnp.broadcast_to(filt_ref[g, pl.ds(s * TAPS + p, 1), :], (ROWS, LANES))

    def first_phase(g):
        slot = lax.rem(g, 2)
        x_copy(g).wait()
        og_copy(g).wait()

        @pl.when(c > 0)
        def _():
            halo_copy(g, c).wait_recv()
            for s in range(3):
                xf[s, BLOCK - 16 : BLOCK, :] = halo[g, s].astype(f32)

        @pl.when(c == 0)
        def _():
            for s in range(3):
                xf[s, BLOCK - 16 : BLOCK, :] = jnp.zeros((16, LANES), f32)

        def widen(k, _):
            come = pl.ds(pl.multiple_of(k * BLOCK, BLOCK), BLOCK)
            for s in range(3):
                xf[s, pl.ds(pl.multiple_of((k + 1) * STRIDE, 8), BLOCK), :] = xin[g, s, come, :].astype(f32)
            ogf[pl.ds(pl.multiple_of(k * STRIDE, 8), BLOCK), :] = ogin[g, come, :].astype(f32)
            return 0

        lax.fori_loop(0, ROWS, widen, 0)

        rate = rate_ref[g]
        decay = spread(jnp.exp(-rate))
        taps = [[tap(g, s, p) for p in range(TAPS)] for s in range(3)]

        def forward(i, carry):
            state, one, two = carry
            now = [xf[s, pl.ds(STRIDE + i, ROWS, stride=STRIDE), :] for s in range(3)]
            q, k, v = [taps[s][0] * now[s] + taps[s][1] * one[s] + taps[s][2] * two[s] for s in range(3)]
            o = ogf[pl.ds(i, ROWS, stride=STRIDE), :]
            product = k * v
            qt[slot, i] = q
            kt[slot, i] = k
            vt[slot, i] = v
            ot[slot, i] = o
            pt[slot, i] = product
            at[slot, i] = o * q
            return (decay * state + product[None], tuple(now), one)

        zero = jnp.zeros((ORDER, ROWS, LANES), f32)
        one = tuple(xf[s, pl.ds(BLOCK - 1, ROWS, stride=STRIDE), :] for s in range(3))
        two = tuple(xf[s, pl.ds(BLOCK - 2, ROWS, stride=STRIDE), :] for s in range(3))
        state, _, _ = steps(forward, (zero, one, two))
        ef[slot] = state

        def back(i, state):
            return decay * state + at[slot, i][None]

        adj_state = steps(back, zero, True)
        eb[slot] = adj_state

        wide = spread(rate) * (-float(BLOCK))
        st_send[g, 0] = jnp.sum(jnp.exp(wide * (ROWS - 1.0 - sublane_f)) * state, axis=1)
        st_send[g, 1] = jnp.sum(jnp.exp(wide * sublane_f) * adj_state, axis=1)

        def later(j, _):
            state_copy(g, 0, j, c).start()
            return 0

        def earlier(j, _):
            state_copy(g, 1, j, c).start()
            return 0

        lax.fori_loop(c + 1, nctx, later, 0)
        lax.fori_loop(0, c, earlier, 0)

    def second_phase(g):
        slot = lax.rem(g, 2)
        rate = rate_ref[g]
        decay = spread(jnp.exp(-rate))
        amp = spread(res_ref[g] * jnp.sqrt(2.0 * rate))
        hop = jnp.exp(-rate * float(span))

        def arrive(j, total):
            state_copy(g, 0, j, j).wait_recv()
            return hop * total + st_recv[g, j]

        def arrive_back(k, total):
            j = nctx - 1 - k
            state_copy(g, 1, j, j).wait_recv()
            return hop * total + st_recv[g, j]

        none = jnp.zeros((ORDER, LANES), f32)
        incoming = lax.fori_loop(0, c, arrive, none)
        outgoing = lax.fori_loop(0, nctx - 1 - c, arrive_back, none)

        def scan(emitted, entry, backward):
            def shift(a, by, fill):
                moved = pltpu.roll(a, ROWS - by if backward else by, 1)
                keep = sublane < ROWS - by if backward else sublane >= by
                return jnp.where(keep, moved, fill)

            total = shift(emitted, 1, spread(entry))
            factor = spread(jnp.exp(-rate * float(BLOCK)))
            for by in (1, 2, 4):
                total = total + factor * shift(total, by, 0.0)
                factor = factor * factor
            return total

        def forward(i, state):
            state = decay * state + pt[slot, i][None]
            long_out = jnp.sum(amp * state, axis=0)
            nat[3, pl.ds(i, ROWS, stride=STRIDE), :] = qt[slot, i] * long_out
            sg[0, i] = ot[slot, i] * long_out
            return state

        steps(forward, scan(ef[slot], incoming, False))

        def back(i, state):
            state = decay * state + at[slot, i][None]
            long_grad = jnp.sum(amp * state, axis=0)
            sg[1, i] = long_grad * vt[slot, i]
            sg[2, i] = long_grad * kt[slot, i]
            return state

        steps(back, scan(eb[slot], outgoing, True), True)

        for s in range(3):
            for r in range(TAPS - 1):
                bsend[g, s, r] = sg[s, r]

        @pl.when(c > 0)
        def _():
            edge_copy(g, c - 1).start()

        taps = [[tap(g, s, p) for p in range(TAPS)] for s in range(3)]

        def short(i, _):
            for s in range(3):
                nat[s, pl.ds(i, ROWS, stride=STRIDE), :] = (
                    taps[s][0] * sg[s, i] + taps[s][1] * sg[s, i + 1] + taps[s][2] * sg[s, i + 2]
                )
            return 0

        steps(short, 0, count=BLOCK - UNROLL)

        def narrow_lay(k, _):
            come = pl.ds(pl.multiple_of(k * STRIDE, 8), BLOCK)
            lay[g, pl.ds(pl.multiple_of(k * BLOCK, BLOCK), BLOCK), :] = nat[3, come, :].astype(bf16)
            return 0

        lax.fori_loop(0, ROWS, narrow_lay, 0)
        lay_copy(g).start()

        @pl.when(c == nctx - 1)
        def _():
            brecv[g] = jnp.zeros((3, TAPS - 1, ROWS, LANES), f32)

        @pl.when(c < nctx - 1)
        def _():
            edge_copy(g, c).wait_recv()

        last = lax.broadcasted_iota(jnp.int32, (ROWS, LANES), 0) == ROWS - 1
        for s in range(3):
            for r in range(TAPS - 1):
                sg[s, BLOCK + r] = jnp.where(
                    last, pltpu.roll(brecv[g, s, r], ROWS - 1, 0), pltpu.roll(sg[s, r], ROWS - 1, 0)
                )
        for i in range(BLOCK - UNROLL, BLOCK):
            short(i, 0)

        def narrow(k, _):
            come = pl.ds(pl.multiple_of(k * STRIDE, 8), BLOCK)
            for s in range(3):
                send[g, s, pl.ds(pl.multiple_of(k * BLOCK, BLOCK), BLOCK), :] = nat[s, come, :].astype(bf16)
            return 0

        lax.fori_loop(0, ROWS, narrow, 0)

        def go(k, _):
            peer = lax.rem(h + lax.rem(k + nch // 2 - 2, nch - 1) + 1, nch)
            out_copy(g, peer, h).start()
            return 0

        lax.fori_loop(1, nch, go, 0)
        own_copy(g).start()

    def both(t, _):
        @pl.when(t < groups)
        def _():
            first_phase(t)

        @pl.when(t > 0)
        def _():
            second_phase(t - 1)

        return 0

    lax.fori_loop(0, groups + 1, both, 0)

    def finish(g, _):
        @pl.when(c < nctx - 1)
        def _():
            halo_copy(g, c).wait_send()

        @pl.when(c > 0)
        def _():
            edge_copy(g, c).wait_send()

        def later(j, _):
            state_copy(g, 0, j, c).wait_send()
            return 0

        def earlier(j, _):
            state_copy(g, 1, j, c).wait_send()
            return 0

        lax.fori_loop(c + 1, nctx, later, 0)
        lax.fori_loop(0, c, earlier, 0)
        lay_copy(g).wait()
        own_copy(g).wait()

        def out(k, _):
            peer = lax.rem(h + k, nch)
            out_copy(g, peer, h).wait_send()
            out_copy(g, peer, peer).wait_recv()
            return 0

        lax.fori_loop(1, nch, out, 0)
        return 0

    lax.fori_loop(0, groups, finish, 0)


def shards(nctx, nch, streams_in, out_grad, decay_rate, residue, short_filter):
    _, span, chans = streams_in.shape
    assert span == ROWS * BLOCK and chans % LANES == 0
    groups = chans // LANES
    token_rows = span // nch
    rate = decay_rate.reshape(groups, LANES, ORDER).swapaxes(1, 2)
    res = residue.reshape(groups, LANES, ORDER).swapaxes(1, 2)
    here = chans // GROUP_SIZE
    local = lax.dynamic_slice_in_dim(short_filter, lax.axis_index("ch") * here, here, 1)
    filt = jnp.repeat(local, GROUP_SIZE, axis=1).reshape(3, groups, LANES, TAPS)
    filt = filt.transpose(1, 0, 3, 2).reshape(groups, 3 * TAPS, LANES)
    turned = (2, BLOCK, ROWS, LANES)
    states = (2, ORDER, ROWS, LANES)
    edge = (groups, 3, TAPS - 1, ROWS, LANES)
    dma = pltpu.SemaphoreType.DMA
    return pl.pallas_call(
        functools.partial(kernel, nctx, nch, groups),
        out_shape=(
            jax.ShapeDtypeStruct((span, chans), bf16),
            jax.ShapeDtypeStruct((3, token_rows, chans * nch), bf16),
        ),
        in_specs=[pl.BlockSpec(memory_space=pl.ANY)] * 2 + [pl.BlockSpec(memory_space=pltpu.VMEM)] * 3,
        out_specs=(pl.BlockSpec(memory_space=pl.ANY),) * 2,
        scratch_shapes=[
            pltpu.VMEM((groups, 3, span, LANES), bf16),
            pltpu.VMEM((groups, span, LANES), bf16),
            pltpu.VMEM((groups, 3, 16, LANES), bf16),
            pltpu.VMEM((3, (ROWS + 1) * STRIDE, LANES), f32),
            pltpu.VMEM((ROWS * STRIDE, LANES), f32),
            *[pltpu.VMEM(turned, f32) for _ in range(6)],
            *[pltpu.VMEM(states, f32) for _ in range(2)],
            pltpu.VMEM((groups, 2, ORDER, LANES), f32),
            pltpu.VMEM((groups, nctx, ORDER, LANES), f32),
            pltpu.VMEM((3, BLOCK + TAPS - 1, ROWS, LANES), f32),
            pltpu.VMEM((4, ROWS * STRIDE, LANES), f32),
            pltpu.VMEM(edge, f32),
            pltpu.VMEM(edge, f32),
            pltpu.VMEM((groups, 3, span, LANES), bf16),
            pltpu.VMEM((groups, span, LANES), bf16),
            dma((2, groups)),
            dma((groups,)),
            dma((groups,)),
            dma((groups, nctx)),
            dma((groups, nctx)),
            dma((groups,)),
            dma((groups,)),
            dma((groups, nch)),
            dma((groups, nch)),
            dma((groups,)),
            dma((groups,)),
        ],
        compiler_params=pltpu.CompilerParams(
            collective_id=0, has_side_effects=True, vmem_limit_bytes=48 * 1024 * 1024
        ),
        cost_estimate=pl.CostEstimate(
            flops=span * chans * 250, bytes_accessed=16 * span * chans, transcendentals=0
        ),
    )(streams_in, out_grad, rate, res, filt)


def solution(mesh):
    return jax.shard_map(
        functools.partial(shards, mesh.shape["ctx"], mesh.shape["ch"]),
        mesh=mesh,
        in_specs=(P(None, "ctx", "ch"), P("ctx", "ch"), P("ch", None), P("ch", None), P()),
        out_specs=(P("ctx", "ch"), P(None, ("ctx", "ch"), None)),
        check_vma=False,
    )
```

time: 602 us -> 167 us (0.28)
  the two profiles are of different devices: /device:TPU:27 before, /device:TPU:13 now
where the time goes in v1:
time: 167 us; the launch traced here: 166 us
  Pallas kernels  154 us (92%)
  local copies, waits for them, and re-layouts  11.1 us (7%)
    pallas_call x1, Pallas kernels, shards(): pl.pallas_call(functools.partial(kernel, nctx, nch, groups), out_shape=(j...  154 us
    unnamed x6, local copies, waits for them, and re-layouts  9.14 us

profile of v1, /device:TPU:13, one launch (start us, length us, event | category | flops | bytes accessed | tf_op | source)
XLA Modules:
  0.0 165.8 jit_solution(1632366317903784815)
XLA Ops:
  0.6 0.0 copy-start
  0.6 0.8 constant_dynamic-slice_fusion
  1.4 0.0 copy-done
  1.5 0.8 bitcast_bitcast_fusion
  2.3 0.1 broadcast_in_dim.3
  2.5 0.1 reshape_reshape.3
  2.6 0.0 copy-start.1
  2.6 1.6 copy-done.1
  4.2 154.0 %shard_map.68 = (bf16[1024,1024]{1,0:T(8,128)(2,1)S(1)}, bf16[3,128,8192]{2,1,0:T(8,128)(2,1)}) custom-call(bf16[3,1024,1024]{2,1,0:T(8,128)(2,1)} %x_hbm.1, bf16[1024,1024]{1,0:T(8,128)(2,1)S(1)} %copy-done.1, f32[8,16,128]{2,1,0:T(8,128)S(1)} %get-tuple-element.3.rate_ref, f32[8,16,128]{2,1,0:T(8,128)S(1)} %get-tuple-element.2.res_ref, ...), custom_call_target="tpu_custom_call" | custom-call | flops 262144000 | bytes 16777216 | tf_op jit(solution)/shard_map/pallas_call | solution.py:391
  158.2 1.3 copy.17
  159.6 6.2 %copy.18 = bf16[3,128,8192]{2,1,0:T(8,128)(2,1)} copy(bf16[3,128,8192]{2,1,0:T(8,128)(2,1)} %get-tuple-element.7) | data formatting | bytes 12582912
  (1 shorter events, 0.0 us)
Async XLA Ops:
  0.6 0.8 copy-start
  2.6 1.6 copy-start.1

commit v2 on v1

v2 whole, which is shorter than its diff:
```python
import functools

import jax
import jax.numpy as jnp
from jax import lax
from jax.experimental import pallas as pl
from jax.experimental.pallas import tpu as pltpu
from jax.sharding import PartitionSpec as P

GROUP_SIZE = 16
TAPS = 3
BLOCK = 128
LANES = 128
ROWS = 8
ORDER = 16
STRIDE = 136
UNROLL = 4
MESH = pl.DeviceIdType.MESH
PARTS = (pl.ds(0, 1), pl.ds(1, 2))
f32 = jnp.float32
bf16 = jnp.bfloat16


def spread(rows):
    return jnp.broadcast_to(rows[:, None, :], (rows.shape[0], ROWS, LANES))


def steps(body, carry, backward=False, count=BLOCK):
    def some(j, carry):
        for u in range(UNROLL):
            i = j * UNROLL + u
            carry = body(count - 1 - i if backward else i, carry)
        return carry

    return lax.fori_loop(0, count // UNROLL, some, carry)


def kernel(
    nctx, nch, groups,
    x_hbm, og_hbm, rate_ref, res_ref, filt_ref,
    lay, sgrad,
    xin, ogin, halo, xf, ogf, filt, qt, kt, vt, ot, pt, at, ef, eb,
    st_send, st_recv, sg, nat, bsend, brecv, send,
    in_sem, halo_send, halo_recv, st_ssem, st_rsem, b_ssem, b_rsem,
    out_ssem, out_rsem, own_sem,
):
    span = x_hbm.shape[1]
    chans = x_hbm.shape[2]
    token_rows = span // nch
    c = lax.axis_index("ctx")
    h = lax.axis_index("ch")

    def lanes(g):
        return pl.ds(pl.multiple_of(g * LANES, LANES), LANES)

    def x_copy(g):
        return pltpu.make_async_copy(x_hbm.at[:, :, lanes(g)], xin.at[g], in_sem.at[0, g])

    def og_copy(g):
        return pltpu.make_async_copy(og_hbm.at[:, lanes(g)], ogin.at[g], in_sem.at[1, g])

    def load(g, _):
        x_copy(g).start()
        og_copy(g).start()
        return 0

    lax.fori_loop(0, groups, load, 0)

    barrier = pltpu.get_barrier_semaphore()

    def greet_ch(k, _):
        pl.semaphore_signal(barrier, inc=1, device_id={"ch": lax.rem(h + k, nch)}, device_id_type=MESH)
        return 0

    def greet_ctx(k, _):
        pl.semaphore_signal(barrier, inc=1, device_id={"ctx": lax.rem(c + k, nctx)}, device_id_type=MESH)
        return 0

    lax.fori_loop(1, nctx, greet_ctx, 0)
    lax.fori_loop(1, nch, greet_ch, 0)

    for s in range(3):
        xf[s, BLOCK - 16 : BLOCK, :] = jnp.zeros((16, LANES), f32)

    def widen(g):
        x_copy(g).wait()
        og_copy(g).wait()

        def block(k, _):
            come = pl.ds(pl.multiple_of(k * BLOCK, BLOCK), BLOCK)
            for s in range(3):
                xf[s, pl.ds(pl.multiple_of((k + 1) * STRIDE, 8), BLOCK), :] = xin[g, s, come, :].astype(f32)
            ogf[pl.ds(pl.multiple_of(k * STRIDE, 8), BLOCK), :] = ogin[g, come, :].astype(f32)
            return 0

        lax.fori_loop(0, ROWS, block, 0)

    widen(0)
    pl.semaphore_wait(barrier, nch + nctx - 2)

    def halo_copy(g, target):
        return pltpu.make_async_remote_copy(
            src_ref=x_hbm.at[:, pl.ds(span - 16, 16), lanes(g)],
            dst_ref=halo.at[g],
            send_sem=halo_send.at[g],
            recv_sem=halo_recv.at[g],
            device_id={"ctx": target},
            device_id_type=MESH,
        )

    @pl.when(c < nctx - 1)
    def _():
        def go(g, _):
            halo_copy(g, c + 1).start()
            return 0

        lax.fori_loop(0, groups, go, 0)

    def state_copy(g, way, peer, slot):
        return pltpu.make_async_remote_copy(
            src_ref=st_send.at[g, way],
            dst_ref=st_recv.at[g, slot],
            send_sem=st_ssem.at[g, peer],
            recv_sem=st_rsem.at[g, slot],
            device_id={"ctx": peer},
            device_id_type=MESH,
        )

    def edge_copy(g, part, target):
        streams = PARTS[part]
        return pltpu.make_async_remote_copy(
            src_ref=bsend.at[g, streams],
            dst_ref=brecv.at[g, streams],
            send_sem=b_ssem.at[part, g],
            recv_sem=b_rsem.at[part, g],
            device_id={"ctx": target},
            device_id_type=MESH,
        )

    def out_copy(g, part, peer, source):
        streams = PARTS[part]
        first = pl.multiple_of(source * chans + g * LANES, LANES)
        return pltpu.make_async_remote_copy(
            src_ref=send.at[g, streams, pl.ds(pl.multiple_of(peer * token_rows, token_rows), token_rows), :],
            dst_ref=sgrad.at[streams, :, pl.ds(first, LANES)],
            send_sem=out_ssem.at[part, g, peer],
            recv_sem=out_rsem.at[part, g, source],
            device_id={"ch": peer},
            device_id_type=MESH,
        )

    def own_copy(g):
        first = pl.multiple_of(h * chans + g * LANES, LANES)
        return pltpu.make_async_copy(
            send.at[g, :, pl.ds(pl.multiple_of(h * token_rows, token_rows), token_rows), :],
            sgrad.at[:, :, pl.ds(first, LANES)],
            own_sem.at[g],
        )

    sublane = lax.broadcasted_iota(jnp.int32, (ORDER, ROWS, LANES), 1)
    sublane_f = sublane.astype(f32)

    first_row = lax.broadcasted_iota(jnp.int32, (ROWS, LANES), 0) == 0
    last_row = lax.broadcasted_iota(jnp.int32, (ROWS, LANES), 0) == ROWS - 1

    def load_taps(slot):
        return [
            [jnp.broadcast_to(filt[slot, s, p : p + 1, :], (ROWS, LANES)) for p in range(TAPS)] for s in range(3)
        ]

    def first_phase(g):
        slot = lax.rem(g, 2)
        all_groups = filt_ref.shape[2]
        base = h * (chans // GROUP_SIZE) + g * (LANES // GROUP_SIZE)
        of_lane = lax.broadcasted_iota(jnp.int32, (all_groups, LANES), 1) // GROUP_SIZE + base
        pick = (lax.broadcasted_iota(jnp.int32, (all_groups, LANES), 0) == of_lane).astype(f32)
        for s in range(3):
            filt[slot, s, 0:TAPS, :] = jnp.dot(
                filt_ref[s], pick, precision=lax.Precision.HIGHEST, preferred_element_type=f32
            )

        rate = rate_ref[:, lanes(g)]
        decay = spread(jnp.exp(-rate))
        taps = load_taps(slot)

        def forward(i, carry):
            state, one, two = carry
            now = [xf[s, pl.ds(STRIDE + i, ROWS, stride=STRIDE), :] for s in range(3)]
            q, k, v = [taps[s][0] * now[s] + taps[s][1] * one[s] + taps[s][2] * two[s] for s in range(3)]
            o = ogf[pl.ds(i, ROWS, stride=STRIDE), :]
            product = k * v
            qt[slot, i] = q
            kt[slot, i] = k
            vt[slot, i] = v
            ot[slot, i] = o
            pt[slot, i] = product
            at[slot, i] = o * q
            return (decay * state + product[None], tuple(now), one)

        zero = jnp.zeros((ORDER, ROWS, LANES), f32)
        one = tuple(xf[s, pl.ds(BLOCK - 1, ROWS, stride=STRIDE), :] for s in range(3))
        two = tuple(xf[s, pl.ds(BLOCK - 2, ROWS, stride=STRIDE), :] for s in range(3))
        state, _, _ = steps(forward, (zero, one, two))
        ef[slot] = state

        @pl.when(c > 0)
        def _():
            halo_copy(g, c).wait_recv()
            before = [halo[g, s].astype(f32) for s in range(3)]
            for i in range(TAPS - 1):
                more = []
                for s in range(3):
                    term = taps[s][i + 1] * jnp.broadcast_to(before[s][15:16], (ROWS, LANES))
                    if i == 0:
                        term = term + taps[s][2] * jnp.broadcast_to(before[s][14:15], (ROWS, LANES))
                    more.append(jnp.where(first_row, term, 0.0))
                q = qt[slot, i] + more[0]
                k = kt[slot, i] + more[1]
                v = vt[slot, i] + more[2]
                change = k * v - pt[slot, i]
                qt[slot, i] = q
                kt[slot, i] = k
                vt[slot, i] = v
                pt[slot, i] = k * v
                at[slot, i] = ot[slot, i] * q
                ef[slot] += spread(jnp.exp(-rate * float(BLOCK - 1 - i))) * change[None]

        wide = spread(rate) * (-float(BLOCK))
        st_send[g, 0] = jnp.sum(jnp.exp(wide * (ROWS - 1.0 - sublane_f)) * ef[slot], axis=1)

        def later(j, _):
            state_copy(g, 0, j, c).start()
            return 0

        lax.fori_loop(c + 1, nctx, later, 0)

        def back(i, state):
            return decay * state + at[slot, i][None]

        adj_state = steps(back, zero, True)
        eb[slot] = adj_state
        st_send[g, 1] = jnp.sum(jnp.exp(wide * sublane_f) * adj_state, axis=1)

        def earlier(j, _):
            state_copy(g, 1, j, c).start()
            return 0

        lax.fori_loop(0, c, earlier, 0)

    def second_phase(g):
        slot = lax.rem(g, 2)
        rate = rate_ref[:, lanes(g)]
        decay = spread(jnp.exp(-rate))
        amp = spread(res_ref[:, lanes(g)] * jnp.sqrt(2.0 * rate))
        taps = load_taps(slot)
        hop = jnp.exp(-rate * float(span))

        def arrive(j, total):
            state_copy(g, 0, j, j).wait_recv()
            return hop * total + st_recv[g, j]

        def arrive_back(k, total):
            j = nctx - 1 - k
            state_copy(g, 1, j, j).wait_recv()
            return hop * total + st_recv[g, j]

        none = jnp.zeros((ORDER, LANES), f32)
        def scan(emitted, entry, backward):
            def shift(a, by, fill):
                moved = pltpu.roll(a, ROWS - by if backward else by, 1)
                keep = sublane < ROWS - by if backward else sublane >= by
                return jnp.where(keep, moved, fill)

            total = shift(emitted, 1, spread(entry))
            factor = spread(jnp.exp(-rate * float(BLOCK)))
            for by in (1, 2, 4):
                total = total + factor * shift(total, by, 0.0)
                factor = factor * factor
            return total

        def short(s, i):
            nat[s, pl.ds(i, ROWS, stride=STRIDE), :] = (
                taps[s][0] * sg[s, i] + taps[s][1] * sg[s, i + 1] + taps[s][2] * sg[s, i + 2]
            )

        def narrow(s, first, last):
            def block(k, _):
                come = pl.ds(pl.multiple_of(k * STRIDE, 8), BLOCK)
                send[g, s, pl.ds(pl.multiple_of(k * BLOCK, BLOCK), BLOCK), :] = nat[s, come, :].astype(bf16)
                return 0

            lax.fori_loop(first, last, block, 0)

        early = nch * (ROWS - 1) // ROWS

        def finish_part(part):
            streams = PARTS[part]
            for s in range(streams.start, streams.start + streams.size):
                for r in range(TAPS - 1):
                    bsend[g, s, r] = sg[s, r]
                    sg[s, BLOCK + r] = pltpu.roll(sg[s, r], ROWS - 1, 0)

            @pl.when(c > 0)
            def _():
                edge_copy(g, part, c - 1).start()

            def some(i, _):
                for s in range(streams.start, streams.start + streams.size):
                    short(s, i)
                return 0

            steps(some, 0)
            for s in range(streams.start, streams.start + streams.size):
                narrow(s, 0, ROWS - 1)

            def go(k, _):
                peer = lax.rem(h + lax.rem(k + nch // 2 - 2, nch - 1) + 1, nch)

                @pl.when(peer < early)
                def _():
                    out_copy(g, part, peer, h).start()

                return 0

            lax.fori_loop(1, nch, go, 0)

        def forward(i, state):
            state = decay * state + pt[slot, i][None]
            long_out = jnp.sum(amp * state, axis=0)
            nat[3, pl.ds(i, ROWS, stride=STRIDE), :] = qt[slot, i] * long_out
            sg[0, i] = ot[slot, i] * long_out
            return state

        incoming = lax.fori_loop(0, c, arrive, none)
        steps(forward, scan(ef[slot], incoming, False))
        finish_part(0)

        def back(i, state):
            state = decay * state + at[slot, i][None]
            long_grad = jnp.sum(amp * state, axis=0)
            sg[1, i] = long_grad * vt[slot, i]
            sg[2, i] = long_grad * kt[slot, i]
            return state

        outgoing = lax.fori_loop(0, nctx - 1 - c, arrive_back, none)
        steps(back, scan(eb[slot], outgoing, True), True)
        finish_part(1)

        def narrow_lay(k, _):
            come = pl.ds(pl.multiple_of(k * STRIDE, 8), BLOCK)
            lay[pl.ds(pl.multiple_of(k * BLOCK, BLOCK), BLOCK), lanes(g)] = nat[3, come, :].astype(bf16)
            return 0

        lax.fori_loop(0, ROWS, narrow_lay, 0)

        @pl.when(c == nctx - 1)
        def _():
            brecv[g] = jnp.zeros((3, TAPS - 1, ROWS, LANES), f32)

        @pl.when(c < nctx - 1)
        def _():
            edge_copy(g, 0, c).wait_recv()
            edge_copy(g, 1, c).wait_recv()

        for s in range(3):
            for r in range(TAPS - 1):
                sg[s, BLOCK + r] = jnp.where(last_row, pltpu.roll(brecv[g, s, r], ROWS - 1, 0), sg[s, BLOCK + r])
            for i in range(BLOCK - TAPS + 1, BLOCK):
                short(s, i)
            narrow(s, ROWS - 1, ROWS)

        def rest(peer, _):
            @pl.when(peer != h)
            def _():
                out_copy(g, 0, peer, h).start()
                out_copy(g, 1, peer, h).start()

            return 0

        lax.fori_loop(early, nch, rest, 0)
        own_copy(g).start()

    def both(t, _):
        @pl.when(t < groups)
        def _():
            first_phase(t)

        @pl.when(t != 1)
        def _():
            second_phase(jnp.maximum(t - 1, 0))

        @pl.when(t + 1 < groups)
        def _():
            widen(t + 1)

        return 0

    lax.fori_loop(0, groups + 1, both, 0)

    def finish(g, _):
        @pl.when(c < nctx - 1)
        def _():
            halo_copy(g, c).wait_send()

        @pl.when(c > 0)
        def _():
            edge_copy(g, 0, c).wait_send()
            edge_copy(g, 1, c).wait_send()

        def later(j, _):
            state_copy(g, 0, j, c).wait_send()
            return 0

        def earlier(j, _):
            state_copy(g, 1, j, c).wait_send()
            return 0

        lax.fori_loop(c + 1, nctx, later, 0)
        lax.fori_loop(0, c, earlier, 0)
        own_copy(g).wait()

        def out(k, _):
            peer = lax.rem(h + k, nch)
            for part in range(2):
                out_copy(g, part, peer, h).wait_send()
                out_copy(g, part, peer, peer).wait_recv()
            return 0

        lax.fori_loop(1, nch, out, 0)
        return 0

    lax.fori_loop(0, groups, finish, 0)


def place(lay, sgrad, lay_out, sgrad_out, sem):
    copies = [pltpu.make_async_copy(sgrad.at[s], sgrad_out.at[s], sem.at[s]) for s in range(3)]
    copies.append(pltpu.make_async_copy(lay, lay_out, sem.at[3]))
    for copy in copies:
        copy.start()
    for copy in copies:
        copy.wait()


def shards(nctx, nch, streams_in, out_grad, decay_rate, residue, short_filter):
    _, span, chans = streams_in.shape
    assert span == ROWS * BLOCK and chans % LANES == 0
    groups = chans // LANES
    token_rows = span // nch
    rate = decay_rate.T
    res = residue.T
    filt = short_filter.transpose(0, 2, 1)
    turned = (2, BLOCK, ROWS, LANES)
    states = (2, ORDER, ROWS, LANES)
    edge = (groups, 3, TAPS - 1, ROWS, LANES)
    dma = pltpu.SemaphoreType.DMA
    whole = pl.BlockSpec(memory_space=pltpu.VMEM)
    held = pl.pallas_call(
        functools.partial(kernel, nctx, nch, groups),
        out_shape=(
            jax.ShapeDtypeStruct((span, chans), bf16),
            jax.ShapeDtypeStruct((3, token_rows, chans * nch), bf16),
        ),
        in_specs=[pl.BlockSpec(memory_space=pltpu.HBM)] * 2 + [whole] * 3,
        out_specs=(whole, pl.BlockSpec(memory_space=pl.ANY)),
        scratch_shapes=[
            pltpu.VMEM((groups, 3, span, LANES), bf16),
            pltpu.VMEM((groups, span, LANES), bf16),
            pltpu.VMEM((groups, 3, 16, LANES), bf16),
            pltpu.VMEM((3, (ROWS + 1) * STRIDE, LANES), f32),
            pltpu.VMEM((ROWS * STRIDE, LANES), f32),
            pltpu.VMEM((2, 3, 8, LANES), f32),
            *[pltpu.VMEM(turned, f32) for _ in range(6)],
            *[pltpu.VMEM(states, f32) for _ in range(2)],
            pltpu.VMEM((groups, 2, ORDER, LANES), f32),
            pltpu.VMEM((groups, nctx, ORDER, LANES), f32),
            pltpu.VMEM((3, BLOCK + TAPS - 1, ROWS, LANES), f32),
            pltpu.VMEM((4, ROWS * STRIDE, LANES), f32),
            pltpu.VMEM(edge, f32),
            pltpu.VMEM(edge, f32),
            pltpu.VMEM((groups, 3, span, LANES), bf16),
            dma((2, groups)),
            dma((groups,)),
            dma((groups,)),
            dma((groups, nctx)),
            dma((groups, nctx)),
            dma((2, groups)),
            dma((2, groups)),
            dma((2, groups, nch)),
            dma((2, groups, nch)),
            dma((groups,)),
        ],
        compiler_params=pltpu.CompilerParams(
            collective_id=0, has_side_effects=True, vmem_limit_bytes=40 * 1024 * 1024
        ),
        cost_estimate=pl.CostEstimate(
            flops=span * chans * 250, bytes_accessed=16 * span * chans, transcendentals=0
        ),
    )(streams_in, out_grad, rate, res, filt)
    return pl.pallas_call(
        place,
        out_shape=tuple(jax.ShapeDtypeStruct(a.shape, a.dtype) for a in held),
        in_specs=[pl.BlockSpec(memory_space=pl.ANY)] * 2,
        out_specs=(pl.BlockSpec(memory_space=pl.ANY),) * 2,
        scratch_shapes=[dma((4,))],
        compiler_params=pltpu.CompilerParams(vmem_limit_bytes=16 * 1024 * 1024),
    )(*held)


def solution(mesh):
    return jax.shard_map(
        functools.partial(shards, mesh.shape["ctx"], mesh.shape["ch"]),
        mesh=mesh,
        in_specs=(P(None, "ctx", "ch"), P("ctx", "ch"), P("ch", None), P("ch", None), P()),
        out_specs=(P("ctx", "ch"), P(None, ("ctx", "ch"), None)),
        check_vma=False,
    )
```

time: 167 us -> 158 us (0.946)
  local copies, waits for them, and re-layouts: 11.1 us -> 4 us
    unnamed x6 -> x8, local copies, waits for them, and re-layouts: 9.14 us -> 4 us
    pallas_call x1, Pallas kernels: 154 us -> 150 us  [shards(): pl.pallas_call(functools.partial(kernel, nctx, nch, groups), out_shape=(j...]
    pallas_call x0 -> x1, Pallas kernels: none -> 3.37 us  [shards(): pl.pallas_call(place, out_shape=tuple((jax.ShapeDtypeStruct(a.shape, a.dt...]
where the time goes in v2:
time: 158 us
  Pallas kernels  153 us (97%)
  local copies, waits for them, and re-layouts  4 us (3%)
    pallas_call x1, Pallas kernels, shards(): pl.pallas_call(functools.partial(kernel, nctx, nch, groups), out_shape=(j...  150 us
    unnamed x8, local copies, waits for them, and re-layouts  4 us
    pallas_call x1, Pallas kernels, shards(): pl.pallas_call(place, out_shape=tuple((jax.ShapeDtypeStruct(a.shape, a.dt...  3.37 us

profile of v2, /device:TPU:13, one launch (start us, length us, event | category | flops | bytes accessed | tf_op | source)
XLA Modules:
  0.0 157.7 jit_solution(14420209502286846253)
XLA Ops:
  0.6 0.0 copy-start
  0.6 1.6 %copy-done = bf16[1024,1024]{1,0:T(8,128)(2,1)S(1)} copy-done((bf16[1024,1024]{1,0:T(8,128)(2,1)S(1)}, bf16[1024,1024]{1,0:T(8,128)(2,1)}, u32[]{:S(2)}) %copy-start) | copy-done | bytes 2097176
  2.2 0.0 copy-start.1
  2.2 0.8 copy-done.1
  3.1 0.0 copy-start.2
  3.1 0.8 copy-done.2
  3.9 0.0 copy-start.3
  3.9 0.7 copy-done.3
  4.6 149.7 %shard_map.68 = (bf16[1024,1024]{1,0:T(8,128)(2,1)S(1)}, bf16[3,128,8192]{2,1,0:T(8,128)(2,1)S(1)}) custom-call(bf16[3,1024,1024]{2,1,0:T(8,128)(2,1)} %x_hbm.1, bf16[1024,1024]{1,0:T(8,128)(2,1)S(1)} %copy-done, f32[16,1024]{1,0:T(8,128)S(1)} %bitcast.3, f32[16,1024]{1,0:T(8,128)S(1)} %bitcast.4, f32[3,3,512]{2,1,0:T(4,128)S(1)} %bitcast.5), custom_call_target="tpu_custom_call" | custom-call | flops 262144000 | bytes 16777216 | tf_op jit(solution)/shard_map/pallas_call | solution.py:457
  154.4 3.4 %shard_map.69 = (bf16[1024,1024]{1,0:T(8,128)(2,1)}, bf16[3,128,8192]{2,1,0:T(8,128)(2,1)}) custom-call(bf16[1024,1024]{1,0:T(8,128)(2,1)S(1)} %get-tuple-element.4.lay, bf16[3,128,8192]{2,1,0:T(8,128)(2,1)S(1)} %get-tuple-element.5.sgrad), custom_call_target="tpu_custom_call" | custom-call | tf_op jit(solution)/shard_map/pallas_call | solution.py:499
Async XLA Ops:
  0.6 1.6 %copy-start = (bf16[1024,1024]{1,0:T(8,128)(2,1)S(1)}, bf16[1024,1024]{1,0:T(8,128)(2,1)}, u32[]{:S(2)}) copy-start(bf16[1024,1024]{1,0:T(8,128)(2,1)} %og_hbm.1) | copy-start | bytes 6291460
  2.2 0.8 copy-start.1
  3.1 0.8 copy-start.2
  3.9 0.7 copy-start.3

commit v3 on v2

--- a/solution.py
+++ b/solution.py
@@ -39,7 +39,7 @@
     nctx, nch, groups,
     x_hbm, og_hbm, rate_ref, res_ref, filt_ref,
     lay, sgrad,
-    xin, ogin, halo, xf, ogf, filt, qt, kt, vt, ot, pt, at, ef, eb,
+    xin, ogin, halo, xf, ogf, all_taps, filt, qt, kt, vt, ot, pt, at, ef, eb,
     st_send, st_recv, sg, nat, bsend, brecv, send,
     in_sem, halo_send, halo_recv, st_ssem, st_rsem, b_ssem, b_rsem,
     out_ssem, out_rsem, own_sem,
@@ -64,7 +64,7 @@
         og_copy(g).start()
         return 0
 
-    lax.fori_loop(0, groups, load, 0)
+    load(0, 0)
 
     barrier = pltpu.get_barrier_semaphore()
 
@@ -79,6 +79,7 @@
     lax.fori_loop(1, nctx, greet_ctx, 0)
     lax.fori_loop(1, nch, greet_ch, 0)
 
+    all_taps[...] = jnp.zeros((16, LANES), f32)
     for s in range(3):
         xf[s, BLOCK - 16 : BLOCK, :] = jnp.zeros((16, LANES), f32)
 
@@ -96,6 +97,7 @@
         lax.fori_loop(0, ROWS, block, 0)
 
     widen(0)
+    lax.fori_loop(1, groups, load, 0)
     pl.semaphore_wait(barrier, nch + nctx - 2)
 
     def halo_copy(g, target):
@@ -110,11 +112,7 @@
 
     @pl.when(c < nctx - 1)
     def _():
-        def go(g, _):
-            halo_copy(g, c + 1).start()
-            return 0
-
-        lax.fori_loop(0, groups, go, 0)
+        halo_copy(0, c + 1).start()
 
     def state_copy(g, way, peer, slot):
         return pltpu.make_async_remote_copy(
@@ -165,19 +163,21 @@
 
     def load_taps(slot):
         return [
-            [jnp.broadcast_to(filt[slot, s, p : p + 1, :], (ROWS, LANES)) for p in range(TAPS)] for s in range(3)
+            [jnp.broadcast_to(filt[slot, pl.ds(s * TAPS + p, 1), :], (ROWS, LANES)) for p in range(TAPS)]
+            for s in range(3)
         ]
 
     def first_phase(g):
         slot = lax.rem(g, 2)
-        all_groups = filt_ref.shape[2]
         base = h * (chans // GROUP_SIZE) + g * (LANES // GROUP_SIZE)
-        of_lane = lax.broadcasted_iota(jnp.int32, (all_groups, LANES), 1) // GROUP_SIZE + base
-        pick = (lax.broadcasted_iota(jnp.int32, (all_groups, LANES), 0) == of_lane).astype(f32)
+        window = base // LANES
         for s in range(3):
-            filt[slot, s, 0:TAPS, :] = jnp.dot(
-                filt_ref[s], pick, precision=lax.Precision.HIGHEST, preferred_element_type=f32
-            )
+            all_taps[s * TAPS : (s + 1) * TAPS, :] = filt_ref[s, :, lanes(window)]
+        of_lane = lax.broadcasted_iota(jnp.int32, (LANES, LANES), 1) // GROUP_SIZE + (base - window * LANES)
+        pick = (lax.broadcasted_iota(jnp.int32, (LANES, LANES), 0) == of_lane).astype(f32)
+        filt[slot] = jnp.dot(
+            all_taps[...], pick, precision=lax.Precision.HIGHEST, preferred_element_type=f32
+        )
 
         rate = rate_ref[:, lanes(g)]
         decay = spread(jnp.exp(-rate))
@@ -393,6 +393,10 @@
         def _():
             widen(t + 1)
 
+            @pl.when(c < nctx - 1)
+            def _():
+                halo_copy(t + 1, c + 1).start()
+
         return 0
 
     lax.fori_loop(0, groups + 1, both, 0)
@@ -433,8 +437,15 @@
 
 
 def place(lay, sgrad, lay_out, sgrad_out, sem):
-    copies = [pltpu.make_async_copy(sgrad.at[s], sgrad_out.at[s], sem.at[s]) for s in range(3)]
-    copies.append(pltpu.make_async_copy(lay, lay_out, sem.at[3]))
+    rows, cut = lay.shape[0] // 4, sgrad.shape[2] // 4
+    copies = []
+    for k in range(4):
+        part = pl.ds(k * cut, cut)
+        for s in range(3):
+            copies.append((sgrad.at[s, :, part], sgrad_out.at[s, :, part]))
+        part = pl.ds(k * rows, rows)
+        copies.append((lay.at[part], lay_out.at[part]))
+    copies = [pltpu.make_async_copy(a, b, sem.at[n]) for n, (a, b) in enumerate(copies)]
     for copy in copies:
         copy.start()
     for copy in copies:
@@ -457,18 +468,19 @@
     held = pl.pallas_call(
         functools.partial(kernel, nctx, nch, groups),
         out_shape=(
-            jax.ShapeDtypeStruct((span, chans), bf16),
-            jax.ShapeDtypeStruct((3, token_rows, chans * nch), bf16),
+            pltpu.VMEM((span, chans), bf16),
+            pltpu.VMEM((3, token_rows, chans * nch), bf16),
         ),
         in_specs=[pl.BlockSpec(memory_space=pltpu.HBM)] * 2 + [whole] * 3,
-        out_specs=(whole, pl.BlockSpec(memory_space=pl.ANY)),
+        out_specs=(whole, whole),
         scratch_shapes=[
             pltpu.VMEM((groups, 3, span, LANES), bf16),
             pltpu.VMEM((groups, span, LANES), bf16),
             pltpu.VMEM((groups, 3, 16, LANES), bf16),
             pltpu.VMEM((3, (ROWS + 1) * STRIDE, LANES), f32),
             pltpu.VMEM((ROWS * STRIDE, LANES), f32),
-            pltpu.VMEM((2, 3, 8, LANES), f32),
+            pltpu.VMEM((16, LANES), f32),
+            pltpu.VMEM((2, 16, LANES), f32),
             *[pltpu.VMEM(turned, f32) for _ in range(6)],
             *[pltpu.VMEM(states, f32) for _ in range(2)],
             pltpu.VMEM((groups, 2, ORDER, LANES), f32),
@@ -490,7 +502,7 @@
             dma((groups,)),
         ],
         compiler_params=pltpu.CompilerParams(
-            collective_id=0, has_side_effects=True, vmem_limit_bytes=40 * 1024 * 1024
+            collective_id=0, has_side_effects=True, vmem_limit_bytes=48 * 1024 * 1024
         ),
         cost_estimate=pl.CostEstimate(
             flops=span * chans * 250, bytes_accessed=16 * span * chans, transcendentals=0
@@ -498,10 +510,10 @@
     )(streams_in, out_grad, rate, res, filt)
     return pl.pallas_call(
         place,
-        out_shape=tuple(jax.ShapeDtypeStruct(a.shape, a.dtype) for a in held),
+        out_shape=tuple(jax.ShapeDtypeStruct(a.shape, bf16) for a in held),
         in_specs=[pl.BlockSpec(memory_space=pl.ANY)] * 2,
         out_specs=(pl.BlockSpec(memory_space=pl.ANY),) * 2,
-        scratch_shapes=[dma((4,))],
+        scratch_shapes=[dma((16,))],
         compiler_params=pltpu.CompilerParams(vmem_limit_bytes=16 * 1024 * 1024),
     )(*held)
 

time: 158 us -> 154 us (0.975)
  local copies, waits for them, and re-layouts: 4 us -> 0 us
    unnamed x8 -> x0, local copies, waits for them, and re-layouts: 4 us -> none
where the time goes in v3:
time: 154 us
  Pallas kernels  153 us (99%)
    pallas_call x1, Pallas kernels, shards(): pl.pallas_call(functools.partial(kernel, nctx, nch, groups), out_shape=(p...  150 us
    pallas_call x1, Pallas kernels, shards(): pl.pallas_call(place, out_shape=tuple((jax.ShapeDtypeStruct(a.shape, bf16...  3.42 us

profile of v3, /device:TPU:13, one launch (start us, length us, event | category | flops | bytes accessed | tf_op | source)
XLA Modules:
  0.0 153.7 jit_solution(122687815177480425)
XLA Ops:
  0.6 149.7 %shard_map.68 = (bf16[1024,1024]{1,0:T(8,128)(2,1)S(1)}, bf16[3,128,8192]{2,1,0:T(8,128)(2,1)S(1)}) custom-call(bf16[3,1024,1024]{2,1,0:T(8,128)(2,1)} %x_hbm.1, bf16[1024,1024]{1,0:T(8,128)(2,1)} %og_hbm.1, f32[16,1024]{1,0:T(8,128)} %bitcast.3, f32[16,1024]{1,0:T(8,128)} %bitcast.4, f32[3,3,512]{2,1,0:T(4,128)} %bitcast.5), custom_call_target="tpu_custom_call" | custom-call | flops 262144000 | bytes 16777216 | tf_op jit(solution)/shard_map/pallas_call | solution.py:468
  150.3 3.4 %shard_map.69 = (bf16[1024,1024]{1,0:T(8,128)(2,1)}, bf16[3,128,8192]{2,1,0:T(8,128)(2,1)}) custom-call(bf16[1024,1024]{1,0:T(8,128)(2,1)S(1)} %get-tuple-element.4.lay, bf16[3,128,8192]{2,1,0:T(8,128)(2,1)S(1)} %get-tuple-element.5.sgrad), custom_call_target="tpu_custom_call" | custom-call | tf_op jit(solution)/shard_map/pallas_call | solution.py:511

commit v4 on v3

--- a/solution.py
+++ b/solution.py
@@ -14,7 +14,7 @@
 ROWS = 8
 ORDER = 16
 STRIDE = 136
-UNROLL = 4
+UNROLL = 8
 MESH = pl.DeviceIdType.MESH
 PARTS = (pl.ds(0, 1), pl.ds(1, 2))
 f32 = jnp.float32
@@ -137,10 +137,9 @@
 
     def out_copy(g, part, peer, source):
         streams = PARTS[part]
-        first = pl.multiple_of(source * chans + g * LANES, LANES)
         return pltpu.make_async_remote_copy(
             src_ref=send.at[g, streams, pl.ds(pl.multiple_of(peer * token_rows, token_rows), token_rows), :],
-            dst_ref=sgrad.at[streams, :, pl.ds(first, LANES)],
+            dst_ref=sgrad.at[streams, source * groups + g],
             send_sem=out_ssem.at[part, g, peer],
             recv_sem=out_rsem.at[part, g, source],
             device_id={"ch": peer},
@@ -148,10 +147,9 @@
         )
 
     def own_copy(g):
-        first = pl.multiple_of(h * chans + g * LANES, LANES)
         return pltpu.make_async_copy(
             send.at[g, :, pl.ds(pl.multiple_of(h * token_rows, token_rows), token_rows), :],
-            sgrad.at[:, :, pl.ds(first, LANES)],
+            sgrad.at[:, h * groups + g],
             own_sem.at[g],
         )
 
@@ -437,19 +435,25 @@
 
 
 def place(lay, sgrad, lay_out, sgrad_out, sem):
-    rows, cut = lay.shape[0] // 4, sgrad.shape[2] // 4
-    copies = []
-    for k in range(4):
-        part = pl.ds(k * cut, cut)
-        for s in range(3):
-            copies.append((sgrad.at[s, :, part], sgrad_out.at[s, :, part]))
-        part = pl.ds(k * rows, rows)
-        copies.append((lay.at[part], lay_out.at[part]))
-    copies = [pltpu.make_async_copy(a, b, sem.at[n]) for n, (a, b) in enumerate(copies)]
-    for copy in copies:
-        copy.start()
-    for copy in copies:
-        copy.wait()
+    slots = sgrad.shape[1]
+
+    def part(j):
+        to = pl.ds(pl.multiple_of(j * LANES, LANES), LANES)
+        return pltpu.make_async_copy(sgrad.at[:, j], sgrad_out.at[:, :, to], sem.at[j])
+
+    def start(j, _):
+        part(j).start()
+        return 0
+
+    def finish(j, _):
+        part(j).wait()
+        return 0
+
+    lax.fori_loop(0, slots, start, 0)
+    whole = pltpu.make_async_copy(lay, lay_out, sem.at[slots])
+    whole.start()
+    lax.fori_loop(0, slots, finish, 0)
+    whole.wait()
 
 
 def shards(nctx, nch, streams_in, out_grad, decay_rate, residue, short_filter):
@@ -469,7 +473,7 @@
         functools.partial(kernel, nctx, nch, groups),
         out_shape=(
             pltpu.VMEM((span, chans), bf16),
-            pltpu.VMEM((3, token_rows, chans * nch), bf16),
+            pltpu.VMEM((3, nch * groups, token_rows, LANES), bf16),
         ),
         in_specs=[pl.BlockSpec(memory_space=pltpu.HBM)] * 2 + [whole] * 3,
         out_specs=(whole, whole),
@@ -510,10 +514,13 @@
     )(streams_in, out_grad, rate, res, filt)
     return pl.pallas_call(
         place,
-        out_shape=tuple(jax.ShapeDtypeStruct(a.shape, bf16) for a in held),
+        out_shape=(
+            jax.ShapeDtypeStruct((span, chans), bf16),
+            jax.ShapeDtypeStruct((3, token_rows, chans * nch), bf16),
+        ),
         in_specs=[pl.BlockSpec(memory_space=pl.ANY)] * 2,
         out_specs=(pl.BlockSpec(memory_space=pl.ANY),) * 2,
-        scratch_shapes=[dma((16,))],
+        scratch_shapes=[dma((nch * groups + 1,))],
         compiler_params=pltpu.CompilerParams(vmem_limit_bytes=16 * 1024 * 1024),
     )(*held)
 

time: 154 us -> 154 us (level)
  no operation moved by 1% of the time
where the time goes in v4:
time: 154 us
  Pallas kernels  153 us (99%)
    pallas_call x1, Pallas kernels, shards(): pl.pallas_call(functools.partial(kernel, nctx, nch, groups), out_shape=(p...  149 us
    pallas_call x1, Pallas kernels, shards(): pl.pallas_call(place, out_shape=(jax.ShapeDtypeStruct((span, chans), bf16...  3.91 us

profile of v4, /device:TPU:13, one launch (start us, length us, event | category | flops | bytes accessed | tf_op | source)
XLA Modules:
  0.0 153.8 jit_solution(13605312363721456915)
XLA Ops:
  0.6 149.3 %shard_map.68 = (bf16[1024,1024]{1,0:T(8,128)(2,1)S(1)}, bf16[3,64,128,128]{3,2,1,0:T(8,128)(2,1)S(1)}) custom-call(bf16[3,1024,1024]{2,1,0:T(8,128)(2,1)} %x_hbm.1, bf16[1024,1024]{1,0:T(8,128)(2,1)} %og_hbm.1, f32[16,1024]{1,0:T(8,128)} %bitcast.3, f32[16,1024]{1,0:T(8,128)} %bitcast.4, f32[3,3,512]{2,1,0:T(4,128)} %bitcast.5), custom_call_target="tpu_custom_call" | custom-call | flops 262144000 | bytes 16777216 | tf_op jit(solution)/shard_map/pallas_call | solution.py:472
  149.9 3.9 %shard_map.69 = (bf16[1024,1024]{1,0:T(8,128)(2,1)}, bf16[3,128,8192]{2,1,0:T(8,128)(2,1)}) custom-call(bf16[1024,1024]{1,0:T(8,128)(2,1)S(1)} %get-tuple-element.4.lay, bf16[3,64,128,128]{3,2,1,0:T(8,128)(2,1)S(1)} %get-tuple-element.5.sgrad), custom_call_target="tpu_custom_call" | custom-call | tf_op jit(solution)/shard_map/pallas_call | solution.py:515

commit v5 on v3

--- a/solution.py
+++ b/solution.py
@@ -14,7 +14,7 @@
 ROWS = 8
 ORDER = 16
 STRIDE = 136
-UNROLL = 4
+UNROLL = 8
 MESH = pl.DeviceIdType.MESH
 PARTS = (pl.ds(0, 1), pl.ds(1, 2))
 f32 = jnp.float32
@@ -314,7 +314,11 @@
                 narrow(s, 0, ROWS - 1)
 
             def go(k, _):
-                peer = lax.rem(h + lax.rem(k + nch // 2 - 2, nch - 1) + 1, nch)
+                peer, low, high = 0, 1, nch // 2
+                while high > 0:
+                    flip, mine = lax.rem(lax.div(k, low), 2), lax.rem(lax.div(h, high), 2)
+                    peer = peer + high * (flip + mine - 2 * flip * mine)
+                    low, high = low * 2, high // 2
 
                 @pl.when(peer < early)
                 def _():

time: 154 us -> 154 us (level)
  no operation moved by 1% of the time
where the time goes in v5:
time: 154 us; the launch traced here: 153 us
  Pallas kernels  153 us (99%)
    pallas_call x1, Pallas kernels, shards(): pl.pallas_call(functools.partial(kernel, nctx, nch, groups), out_shape=(p...  149 us
    pallas_call x1, Pallas kernels, shards(): pl.pallas_call(place, out_shape=tuple((jax.ShapeDtypeStruct(a.shape, bf16...  3.42 us

profile of v5, /device:TPU:13, one launch (start us, length us, event | category | flops | bytes accessed | tf_op | source)
XLA Modules:
  0.0 153.2 jit_solution(13123759488422693555)
XLA Ops:
  0.6 149.1 %shard_map.68 = (bf16[1024,1024]{1,0:T(8,128)(2,1)S(1)}, bf16[3,128,8192]{2,1,0:T(8,128)(2,1)S(1)}) custom-call(bf16[3,1024,1024]{2,1,0:T(8,128)(2,1)} %x_hbm.1, bf16[1024,1024]{1,0:T(8,128)(2,1)} %og_hbm.1, f32[16,1024]{1,0:T(8,128)} %bitcast.3, f32[16,1024]{1,0:T(8,128)} %bitcast.4, f32[3,3,512]{2,1,0:T(4,128)} %bitcast.5), custom_call_target="tpu_custom_call" | custom-call | flops 262144000 | bytes 16777216 | tf_op jit(solution)/shard_map/pallas_call | solution.py:472
  149.8 3.4 %shard_map.69 = (bf16[1024,1024]{1,0:T(8,128)(2,1)}, bf16[3,128,8192]{2,1,0:T(8,128)(2,1)}) custom-call(bf16[1024,1024]{1,0:T(8,128)(2,1)S(1)} %get-tuple-element.4.lay, bf16[3,128,8192]{2,1,0:T(8,128)(2,1)S(1)} %get-tuple-element.5.sgrad), custom_call_target="tpu_custom_call" | custom-call | tf_op jit(solution)/shard_map/pallas_call | solution.py:515
